TPU v7x, 32 devices: a whole 2x2x4 slice. The times are simulated.
32 devices in a mesh: grp: 8 (over y, x, core), dev: 4 (over z).
Axes of the slice: x: 2, y: 2, z: 4, core: 2. Of those that a mesh axis runs over, the one named last changes fastest.
Arguments:
- design: float32 [16384, 1024], P(('grp', 'dev')), as said below
- observed: float32 [16384], P(('grp', 'dev')), may hold values from -6 to 6
- row_weight: float32 [16384], P(('grp', 'dev')), may hold values from 0.3 to 3
- arc_of_row: int32 [16384, 1], P(('grp', 'dev')), may hold values from 0 to 7, as said below
- prior_factor: float32 [1024, 1024], P('dev'), as said below
- prior_rhs: float32 [1024], P('dev'), may hold values from -6 to 6
Outputs:
- new_factor: float32 [1024, 1024], P('dev')
- new_rhs: float32 [1024], P('dev')
Inputs may be any that keep to these rules, and one draw needn't show every extreme that they name: `arc_of_row`: arc numbers count within a group of 4 devices along dev; arc a of a group is owned by the device of index a // 2 in that group. Among the rows of one device no arc stands more than 96 times. In every group the arcs of one owner stand exactly 96 times among the rows of every device of that group. `prior_factor`: upper triangular with diagonal between 1 and 2. `design`: entries below 1 in magnitude.
All inputs are finite; a program needn't handle non-finite values.
Results may differ from a plain program's by a relative error of at most 0.0013.
Values sent between devices are 32-bit elements; how exact they have to be, the bound alone decides.
A program may use at most 128 MiB of HBM per device.

v0:
```python
import jax
import jax.numpy as jnp
from jax import lax
from jax.sharding import PartitionSpec as P

ARCS_DEV = 2


bias_prior = 1.0


def inner(left, right):
    return lax.dot_general(
        left,
        right,
        (((0,), (0,)), ((), ())),
        precision=lax.Precision.HIGHEST,
        preferred_element_type=jnp.float32,
    )


def on_device(design, observed, row_weight, arc_of_row, prior_factor, prior_rhs):
    n_dev = lax.axis_size("dev")
    row_count, width = design.shape
    arcs_group = ARCS_DEV * n_dev
    arc_index = arc_of_row[:, 0]
    onehot = (arc_index[:, None] == jnp.arange(arcs_group, dtype=jnp.int32)[None, :]).astype(
        jnp.float32
    )
    weighted = row_weight[:, None] * design
    scaled_obs = row_weight * observed
    most = max(row_count * 3 // (2 * arcs_group), 2)
    slots = ARCS_DEV * most
    owner_dev = arc_index // ARCS_DEV
    within_arc = arc_index % ARCS_DEV
    earlier = jnp.tril(jnp.ones((row_count, row_count), jnp.float32), -1)
    row_rank = jnp.sum(
        jnp.dot(earlier, onehot, precision=lax.Precision.HIGHEST) * onehot, axis=1
    ).astype(jnp.int32)
    target = owner_dev * slots + within_arc * most + row_rank
    buffer = (
        jnp.zeros((n_dev * slots, width), jnp.float32)
        .at[target]
        .set(weighted)
        .reshape(n_dev, slots, width)
    )
    pairs = jnp.stack([row_weight, scaled_obs], axis=1)
    side_info = (
        jnp.zeros((n_dev * slots, 2), jnp.float32).at[target].set(pairs).reshape(n_dev, slots, 2)
    )
    side_info = jnp.transpose(side_info, (0, 2, 1))
    got_rows, got_side = (
        lax.all_to_all(buffer, "dev", split_axis=0, concat_axis=0, tiled=True),
        lax.all_to_all(side_info, "dev", split_axis=0, concat_axis=0, tiled=True),
    )
    data_rows = got_rows.reshape(n_dev * slots, width)
    weights = got_side[:, 0, :].reshape(n_dev, ARCS_DEV, most)
    obs_got = got_side[:, 1, :].reshape(n_dev, ARCS_DEV, most)
    data_obs = got_side[:, 1, :].reshape(-1)
    arc_sum = jnp.einsum(
        "sam,samp->ap",
        weights,
        got_rows.reshape(n_dev, ARCS_DEV, most, width),
        precision=lax.Precision.HIGHEST,
    )
    total = jnp.sum(weights * weights, axis=(0, 2)) + bias_prior
    obs_sum = jnp.sum(weights * obs_got, axis=(0, 2))
    scaled_arcs = arc_sum / total[:, None]
    include = (lax.axis_index("grp") == 0).astype(jnp.float32)
    prior_local = prior_factor * include
    projected = (
        inner(data_rows, data_obs) + inner(prior_local, prior_rhs) - inner(arc_sum, obs_sum / total)
    )
    projected = lax.psum(projected, ("grp", "dev"))
    block = lax.psum_scatter(
        inner(data_rows, data_rows) + inner(prior_local, prior_local) - inner(scaled_arcs, arc_sum),
        "dev",
        scatter_dimension=0,
        tiled=True,
    )
    block = lax.psum(block, "grp")
    gram = lax.all_gather(block, "dev", axis=0, tiled=True)
    lower = jnp.linalg.cholesky(gram)
    solved = lax.linalg.triangular_solve(lower, projected[:, None], left_side=True, lower=True)[
        :, 0
    ]
    share = width // n_dev
    first_row = lax.axis_index("dev") * share
    factor_rows = lax.dynamic_slice_in_dim(lower, first_row, share, 1).T
    rhs_rows = lax.dynamic_slice_in_dim(solved, first_row, share, 0)
    return (factor_rows, rhs_rows)


def solution(mesh):
    placed = (
        P(("grp", "dev"), None),
        P(("grp", "dev")),
        P(("grp", "dev")),
        P(("grp", "dev"), None),
        P("dev", None),
        P("dev"),
    )
    return jax.shard_map(
        on_device, mesh=mesh, in_specs=placed, out_specs=(P("dev", None), P("dev")), check_vma=False
    )
```

profile of v0, /device:TPU:0, one launch (start us, length us, event | category | flops | bytes accessed | tf_op | source)
XLA Modules:
  0.0 684.5 jit_solution(5628965382830347020)
XLA Ops:
  13.6 6.3 all-to-all-start.1
  19.9 5.3 scatter_custom_fusion
  25.5 4.8 all-to-all-start
  30.8 7.1 %fusion.29 = f32[1024,1024]{0,1:T(8,128)} fusion(f32[256,1024]{1,0:T(8,128)} %param.10, f32[]{:T(128)S(6)} %convert_element_type.19), kind=kOutput, calls=%fused_computation.68 | convolution fusion | flops 3221487616 | bytes 5242884 | tf_op jit(solution)/shard_map/dot_general | solution.py:13
  38.2 62.2 %all-to-all-done = f32[4,192,1024]{2,1,0:T(8,128)S(1)} async-done(((f32[4,192,1024]{2,1,0:T(8,128)}), f32[4,192,1024]{2,1,0:T(8,128)S(1)}, u32[]{:S(2)}, u32[]{:S(2)}) %all-to-all-start) | async-done | bytes 3145760 | tf_op jit(solution)/shard_map/all_to_all | solution.py:53
  102.2 11.3 %fusion.102 = f32[1024,1024,1]{0,1,2:T(8,128)S(1)} fusion(f32[4,192,1024]{2,1,0:T(8,128)S(1)} %all-to-all-done), kind=kOutput, calls=%fused_computation.226 | convolution fusion | flops 9663676416 | bytes 7340032 | tf_op jit(solution)/shard_map/dot_general | solution.py:13
  113.5 5.4 fusion.1
  119.0 76.0 %reduce-scatter.2.cloned.1.call-done = f32[256,1024]{0,1:T(8,128)} async-done(((f32[1024,1024]{0,1:T(8,128)}), f32[256,1024]{0,1:T(8,128)}) %reduce-scatter.2.cloned.1.call-update) | async-done | bytes 1048592 | tf_op jit(solution)/shard_map/reduce_scatter | solution.py:75
  195.0 60.6 %all-reduce.3.cloned.1.call-done = f32[256,1024]{0,1:T(8,128)} async-done(((f32[256,1024]{0,1:T(8,128)}), f32[256,1024]{0,1:T(8,128)}) %all-reduce.3.cloned.1.call-update) | async-done | bytes 1048592 | tf_op jit(solution)/shard_map/psum | solution.py:81
  259.8 43.1 %psum.15 = f32[1024]{0:T(1024)S(1)} all-reduce(f32[1024]{0:T(1024)S(1)} %add_subtract_fusion), channel_id=1, replica_groups=mesh['grp'=8,'dev'=4] {'grp','dev'}, use_global_device_ids=true, to_apply=%region_25.26 | all-reduce | flops 1024 | bytes 8192 | tf_op jit(solution)/shard_map/psum | solution.py:74
  302.9 35.2 %all-gather.2.cloned.1.call-done = f32[1024,1024]{0,1:T(8,128)} async-done(((f32[256,1024]{0,1:T(8,128)}), f32[1024,1024]{0,1:T(8,128)}) %all-gather.2.cloned.1.call-update) | async-done | bytes 4194320 | tf_op jit(solution)/shard_map/all_gather | solution.py:82
  338.1 5.5 copy.37
  343.6 4.4 fusion
  350.0 11.7 %cholesky.223 = f32[128,128]{1,0:T(8,128)S(1)} custom-call(f32[128,128]{1,0:T(8,128)S(1)} %cholesky.580), custom_call_target="Cholesky" | custom-call | tf_op jit(solution)/shard_map/jit(cholesky)/cholesky | solution.py:83
  364.3 9.8 %custom-call.62 = f32[1,128,128]{1,2,0:T(8,128)S(1)} custom-call(f32[1,128,128]{2,1,0:T(8,128)S(1)} %get-tuple-element.57), custom_call_target="InvertDiagBlocksLowerTriangular" | custom-call | tf_op jit(solution)/shard_map/jit(cholesky)/cholesky | solution.py:83
  378.0 12.1 %cholesky.244 = f32[128,128]{1,0:T(8,128)S(1)} custom-call(f32[128,128]{1,0:T(8,128)S(1)} %cholesky.584), custom_call_target="Cholesky" | custom-call | tf_op jit(solution)/shard_map/jit(cholesky)/cholesky | solution.py:83
  390.8 9.8 %custom-call.63 = f32[1,128,128]{1,2,0:T(8,128)S(1)} custom-call(f32[1,128,128]{2,1,0:T(8,128)S(1)} %get-tuple-element.54), custom_call_target="InvertDiagBlocksLowerTriangular" | custom-call | tf_op jit(solution)/shard_map/jit(cholesky)/cholesky | solution.py:83
  403.9 11.7 %cholesky.468 = f32[128,128]{1,0:T(8,128)S(1)} custom-call(f32[128,128]{1,0:T(8,128)S(1)} %cholesky.589), custom_call_target="Cholesky" | custom-call | tf_op jit(solution)/shard_map/jit(cholesky)/cholesky | solution.py:83
  416.9 9.8 %custom-call.64 = f32[1,128,128]{1,2,0:T(8,128)S(1)} custom-call(f32[1,128,128]{2,1,0:T(8,128)S(1)} %get-tuple-element.51), custom_call_target="InvertDiagBlocksLowerTriangular" | custom-call | tf_op jit(solution)/shard_map/jit(cholesky)/cholesky | solution.py:83
  430.3 11.9 %cholesky.487 = f32[128,128]{1,0:T(8,128)S(1)} custom-call(f32[128,128]{1,0:T(8,128)S(1)} %cholesky.594), custom_call_target="Cholesky" | custom-call | tf_op jit(solution)/shard_map/jit(cholesky)/cholesky | solution.py:83
  443.5 9.8 %custom-call.65 = f32[1,128,128]{1,2,0:T(8,128)S(1)} custom-call(f32[1,128,128]{2,1,0:T(8,128)S(1)} %get-tuple-element.48), custom_call_target="InvertDiagBlocksLowerTriangular" | custom-call | tf_op jit(solution)/shard_map/jit(cholesky)/cholesky | solution.py:83
  456.8 11.7 %cholesky.506 = f32[128,128]{1,0:T(8,128)S(1)} custom-call(f32[128,128]{1,0:T(8,128)S(1)} %cholesky.599), custom_call_target="Cholesky" | custom-call | tf_op jit(solution)/shard_map/jit(cholesky)/cholesky | solution.py:83
  469.8 10.2 %custom-call.66 = f32[1,128,128]{1,2,0:T(8,128)S(1)} custom-call(f32[1,128,128]{2,1,0:T(8,128)S(1)} %get-tuple-element.45), custom_call_target="InvertDiagBlocksLowerTriangular" | custom-call | tf_op jit(solution)/shard_map/jit(cholesky)/cholesky | solution.py:83
  483.3 11.7 %cholesky.526 = f32[128,128]{1,0:T(8,128)S(1)} custom-call(f32[128,128]{1,0:T(8,128)S(1)} %cholesky.604), custom_call_target="Cholesky" | custom-call | tf_op jit(solution)/shard_map/jit(cholesky)/cholesky | solution.py:83
  496.3 9.8 %custom-call.67 = f32[1,128,128]{1,2,0:T(8,128)S(1)} custom-call(f32[1,128,128]{2,1,0:T(8,128)S(1)} %get-tuple-element.42), custom_call_target="InvertDiagBlocksLowerTriangular" | custom-call | tf_op jit(solution)/shard_map/jit(cholesky)/cholesky | solution.py:83
  509.1 11.9 %cholesky.546 = f32[128,128]{1,0:T(8,128)S(1)} custom-call(f32[128,128]{1,0:T(8,128)S(1)} %cholesky.609), custom_call_target="Cholesky" | custom-call | tf_op jit(solution)/shard_map/jit(cholesky)/cholesky | solution.py:83
  522.3 9.8 %custom-call.68 = f32[1,128,128]{1,2,0:T(8,128)S(1)} custom-call(f32[1,128,128]{2,1,0:T(8,128)S(1)} %get-tuple-element.39), custom_call_target="InvertDiagBlocksLowerTriangular" | custom-call | tf_op jit(solution)/shard_map/jit(cholesky)/cholesky | solution.py:83
  534.7 11.7 %cholesky.564 = f32[128,128]{1,0:T(8,128)S(1)} custom-call(f32[128,128]{1,0:T(8,128)S(1)} %convolution_subtract_fusion.6), custom_call_target="Cholesky" | custom-call | tf_op jit(solution)/shard_map/jit(cholesky)/cholesky | solution.py:83
  553.4 4.8 fusion.2
  559.6 27.6 %while.1 = (s32[]{:T(128)}, f32[1024,1024]{1,0:T(8,128)}, s32[8,2]{0,1:T(2,128)S(1)}, f32[8,128,128]{2,1,0:T(8,128)}, s32[]{:T(128)}) while((s32[]{:T(128)}, f32[1024,1024]{1,0:T(8,128)}, s32[8,2]{0,1:T(2,128)S(1)}, f32[8,128,128]{2,1,0:T(8,128)}, s32[]{:T(128)}) %tuple.70), condition=%wide.while_cond, body=%wide.while_body.sunk | while | flops 2 | bytes 132205 | solution.py:84
  560.3 2.9 bitcast_dynamic-update-slice_fusion.2
  587.3 79.4 %custom-call.69 = f32[8,128,128]{1,2,0:T(8,128)S(1)} custom-call(f32[8,128,128]{2,1,0:T(8,128)} %get-tuple-element.9), custom_call_target="InvertDiagBlocksLowerTriangular" | custom-call | tf_op jit(solution)/shard_map/triangular_solve | solution.py:84
  (116 shorter events, 87.5 us)
Async XLA Ops:
  7.2 248.5 %copy-start = (f32[256]{0:T(256)S(1)}, f32[256]{0:T(256)}, u32[]{:S(2)}) copy-start(f32[256]{0:T(256)} %param.11) | copy-start | bytes 3076
  13.6 11.9 %all-to-all-start.1 = ((f32[4,2,192]{2,1,0:T(2,128)}), f32[4,2,192]{2,1,0:T(2,128)S(1)}, u32[]{:S(2)}, u32[]{:S(2)}) async-start(f32[4,2,192]{2,1,0:T(2,128)} %bitcast.8), calls=%async_computation.1 | async-start | bytes 16384 | tf_op jit(solution)/shard_map/all_to_all | solution.py:54
  25.5 74.9 %all-to-all-start = ((f32[4,192,1024]{2,1,0:T(8,128)}), f32[4,192,1024]{2,1,0:T(8,128)S(1)}, u32[]{:S(2)}, u32[]{:S(2)}) async-start(f32[4,192,1024]{2,1,0:T(8,128)} %bitcast.231), calls=%async_computation | async-start | bytes 6291456 | tf_op jit(solution)/shard_map/all_to_all | solution.py:53
  30.3 164.6 %reduce-scatter.2.cloned.1.call-start = ((), (), s32[]{:S(2)}) async-start(), calls=%async_computation.3 | async-start | bytes 5242880 | tf_op jit(solution)/shard_map/reduce_scatter | solution.py:75
  102.2 11.3 %copy-start.1 = (f32[1024,1024]{0,1:T(8,128)S(1)}, f32[1024,1024]{0,1:T(8,128)}, u32[]{:S(2)}) copy-start(f32[1024,1024]{0,1:T(8,128)} %fusion.29) | copy-start | bytes 12582916
  118.9 136.7 %all-reduce.3.cloned.1.call-start = ((), (), s32[]{:S(2)}) async-start(), calls=%async_computation.4 | async-start | bytes 2097152 | tf_op jit(solution)/shard_map/psum | solution.py:81
  195.0 143.1 %all-gather.2.cloned.1.call-start = ((), (), s32[]{:S(2)}) async-start(), calls=%async_computation.5 | async-start | bytes 5242880 | tf_op jit(solution)/shard_map/all_gather | solution.py:82
  348.1 1.9 copy-start.2
Sparse Core Ops, SparseCore 0:
  119.0 75.8 reduce-scatter.1
  198.4 57.1 all-reduce.2
  257.2 80.8 all-gather.1
where the time goes:
time: 690 us; the launch traced here: 684 us
  other arithmetic  269 us (39%)
  waiting for transfers between devices  234 us (34%)
  matrix products  64.5 us (9%)
  blocking collectives  43.1 us (6%)
  local copies, waits for them, and re-layouts  42.7 us (6%)
  between operations  19.2 us (3%)
  starting transfers between devices  11.7 us (2%)
    another operation x30, other arithmetic, on_device(): lower = jnp.linalg.cholesky(gram)  173 us
    another operation x3, other arithmetic, on_device(): lax.linalg.triangular_solve(lower, projected[:, None], left_side=True, lo...  84.2 us
    reduce_scatter x1, waiting for transfers between devices, on_device(): lax.psum_scatter(inner(data_rows, data_rows) + inner(prior_local, prior_l...  76 us
    all_to_all x1, waiting for transfers between devices, on_device(): lax.all_to_all(buffer, 'dev', split_axis=0, concat_axis=0, tiled=True)  62.2 us
    psum x1, waiting for transfers between devices, on_device(): block = lax.psum(block, 'grp')  60.6 us
    psum x1, blocking collectives, on_device(): projected = lax.psum(projected, ('grp', 'dev'))  43.1 us
    all_gather x1, waiting for transfers between devices, on_device(): gram = lax.all_gather(block, 'dev', axis=0, tiled=True)  35.2 us
    another operation x24, local copies, waits for them, and re-layouts  27.6 us
  transfers between devices with their start and end apart: 5, of which 5 were waited for; matrix products, arithmetic and copies ran while one was open for 2% of the time, Pallas kernels for 0%

commit v1 on v0

v1 whole, which is shorter than its diff:
```python
import functools

import jax
import jax.numpy as jnp
from jax import lax
from jax.experimental import pallas as pl
from jax.experimental.pallas import tpu as pltpu
from jax.sharding import PartitionSpec as P

ARCS_DEV = 2
BLOCK = 128
SLAB = 8

bias_prior = 1.0


def inner(left, right):
    return lax.dot_general(
        left,
        right,
        (((0,), (0,)), ((), ())),
        precision=lax.Precision.HIGH,
        preferred_element_type=jnp.float32,
    )


def dot(left, right, contract):
    return lax.dot_general(
        left,
        right,
        (((contract,), (0,)), ((), ())),
        precision=lax.Precision.HIGHEST,
        preferred_element_type=jnp.float32,
    )


def lane(x, c):
    return jnp.broadcast_to(x[:, c : c + 1], (SLAB, BLOCK))


def row(x, i):
    return jnp.broadcast_to(x[i : i + 1, :], (SLAB, BLOCK))


def factor_block(block, beside):
    slabs = BLOCK // SLAB
    sub = lax.broadcasted_iota(jnp.int32, (SLAB, BLOCK), 0)
    col = lax.broadcasted_iota(jnp.int32, (SLAB, BLOCK), 1)
    main = [block[SLAB * m : SLAB * (m + 1), :] for m in range(slabs)]
    side = [(col == sub + SLAB * m).astype(jnp.float32) for m in range(slabs)]
    upper, inverse = [], []
    for k in range(slabs):
        a, s = main[k], side[k]
        coef = [lane(a, SLAB * k + j) for j in range(SLAB)]
        up, inv = a, s
        for i in range(SLAB):
            here = sub == i
            pivot = coef[i]
            value = row(pivot, i)
            root = lax.rsqrt(value)
            root = root * (1.5 - 0.5 * value * root * root)
            recip = root * root
            row_a, row_s = row(a, i), row(s, i)
            up = jnp.where(here, row_a * root, up)
            inv = jnp.where(here, row_s * root, inv)
            for j in range(i + 1, SLAB):
                e = row(coef[j], i) * recip
                coef[j] = jnp.where(here, e, coef[j] - pivot * e)
            z_a, z_s = row_a * recip, row_s * recip
            a = jnp.where(here, z_a, a - pivot * z_a)
            s = jnp.where(here, z_s, s - pivot * z_s)
        upper.append(jnp.where(col >= sub + SLAB * k, up, 0.0))
        inverse.append(inv)
        rows_a = [row(a, j) for j in range(SLAB)]
        rows_s = [row(s, j) for j in range(SLAB)]
        for m in range(k + 1, slabs):
            c = [lane(main[m], SLAB * k + j) for j in range(SLAB)]
            for j in range(SLAB):
                main[m] = main[m] - c[j] * rows_a[j]
                side[m] = side[m] - c[j] * rows_s[j]
        beside(k)
    return jnp.concatenate(upper, axis=0), jnp.concatenate(inverse, axis=0)


def chunks(wide):
    out, at = [], 0
    while at < wide:
        step = min(2 * BLOCK, wide - at)
        out.append((at, step))
        at += step
    return out


def cholesky_kernel(g_ref, u_ref, ahead, panel):
    width, wide = g_ref.shape
    panels = width // BLOCK
    parts = chunks(wide)
    u_ref[...] = jnp.zeros_like(u_ref)
    ahead[...] = g_ref[0:BLOCK, :]

    def body(p, carry):
        here = pl.ds(pl.multiple_of(p * BLOCK, BLOCK), BLOCK)
        before = pl.ds(pl.multiple_of(jnp.maximum(p - 1, 0) * BLOCK, BLOCK), BLOCK)
        after = pl.ds(pl.multiple_of(jnp.minimum(p + 1, panels - 1) * BLOCK, BLOCK), BLOCK)
        left = u_ref[before, here]
        diag = ahead[:, here] - dot(left, left, 0)
        for at, step in parts:
            cut = pl.ds(at, step)
            panel[:, cut] = ahead[:, cut] - dot(left, u_ref[before, cut], 0)

        def beside(k):
            if k % 3 == 0 and k // 3 < len(parts):
                at, step = parts[k // 3]
                cut = pl.ds(at, step)
                ahead[:, cut] = g_ref[after, cut] - dot(
                    u_ref[:, after], u_ref[:, cut], 0
                )

        upper, inverse = factor_block(diag, beside)
        for at, step in parts:
            cut = pl.ds(at, step)
            new = dot(inverse, panel[:, cut], 1)
            columns = lax.broadcasted_iota(jnp.int32, (BLOCK, step), 1) + at
            new = jnp.where(columns >= p * BLOCK, new, 0.0)
            u_ref[here, cut] = new
        u_ref[here, here] = upper
        return carry

    lax.fori_loop(0, panels, body, 0)


def cholesky(gram):
    width, wide = gram.shape
    return pl.pallas_call(
        cholesky_kernel,
        out_shape=jax.ShapeDtypeStruct((width, wide), jnp.float32),
        in_specs=[pl.BlockSpec(memory_space=pltpu.VMEM)],
        out_specs=pl.BlockSpec(memory_space=pltpu.VMEM),
        scratch_shapes=[
            pltpu.VMEM((BLOCK, wide), jnp.float32),
            pltpu.VMEM((BLOCK, wide), jnp.float32),
        ],
        compiler_params=pltpu.CompilerParams(vmem_limit_bytes=40 * 2**20),
    )(gram)


def on_device(design, observed, row_weight, arc_of_row, prior_factor, prior_rhs):
    n_dev, n_grp = lax.axis_size("dev"), lax.axis_size("grp")
    dev, grp = lax.axis_index("dev"), lax.axis_index("grp")
    row_count, width = design.shape
    arcs_group = ARCS_DEV * n_dev
    column = row_weight[:, None]
    scaled_obs = column * observed[:, None]
    pad = jnp.zeros((row_count, BLOCK - 2), jnp.float32)
    weighted = jnp.concatenate([column * design, scaled_obs, column, pad], axis=1)
    onehot = arc_of_row == jnp.arange(arcs_group, dtype=jnp.int32)[None, :]
    arcs = lax.psum(inner(jnp.where(onehot, column, 0.0), weighted), "dev")
    arcs = lax.dynamic_slice_in_dim(arcs, dev * ARCS_DEV, ARCS_DEV, 0)
    total = arcs[:, width + 1 : width + 2] + bias_prior
    prior_rows = width // (n_dev * n_grp)
    prior = jnp.concatenate(
        [prior_factor, prior_rhs[:, None], jnp.zeros((prior_factor.shape[0], BLOCK - 1), jnp.float32)],
        axis=1,
    )
    prior = lax.dynamic_slice_in_dim(prior, grp * prior_rows, prior_rows, 0)
    left = jnp.concatenate([weighted[:, :width], prior[:, :width], -arcs[:, :width] / total], axis=0)
    right = jnp.concatenate([weighted, prior, arcs], axis=0)
    gram = lax.psum(inner(left, right), ("grp", "dev"))
    factor = cholesky(gram)
    share = width // n_dev
    rows = lax.dynamic_slice_in_dim(factor, dev * share, share, 0)
    return rows[:, :width], rows[:, width]


def solution(mesh):
    placed = (
        P(("grp", "dev"), None),
        P(("grp", "dev")),
        P(("grp", "dev")),
        P(("grp", "dev"), None),
        P("dev", None),
        P("dev"),
    )
    return jax.shard_map(
        on_device, mesh=mesh, in_specs=placed, out_specs=(P("dev", None), P("dev")), check_vma=False
    )
```

time: 690 us -> 262 us (0.38)
  other arithmetic: 269 us -> 3.27 us
  waiting for transfers between devices: 234 us -> 143 us
  Pallas kernels: 0 us -> 60.6 us
  matrix products: 64.5 us -> 10 us
  local copies, waits for them, and re-layouts: 42.7 us -> 9.38 us
  blocking collectives: 43.1 us -> 21.2 us
  starting transfers between devices: 11.7 us -> 0.04 us
    another operation x34 -> x0, other arithmetic: 257 us -> none  [the longest x30 173 us: on_device(): lower = jnp.linalg.cholesky(gram)]
    psum x1, waiting for transfers between devices: 60.6 us -> 143 us  [on_device(): gram = lax.psum(inner(left, right), ('grp', 'dev'))]
    reduce_scatter x1 -> x0, waiting for transfers between devices: 76 us -> none  [on_device(): lax.psum_scatter(inner(data_rows, data_rows) + inner(prior_local, prior_l...]
    all_to_all x2 -> x0, waiting for transfers between devices: 62.5 us -> none  [the longest x1 62.2 us: on_device(): lax.all_to_all(buffer, 'dev', split_axis=0, concat_axis=0, tiled=True)]
    pallas_call x0 -> x1, Pallas kernels: none -> 60.6 us  [cholesky(): pl.pallas_call(cholesky_kernel, out_shape=jax.ShapeDtypeStruct((width, wi...]
    all_gather x1 -> x0, waiting for transfers between devices: 35.2 us -> none  [on_device(): gram = lax.all_gather(block, 'dev', axis=0, tiled=True)]
    another operation x29 -> x0, matrix products: 33.6 us -> none  [the longest x14 23.1 us: on_device(): lower = jnp.linalg.cholesky(gram)]
    another operation x36 -> x0, local copies, waits for them, and re-layouts: 30.5 us -> none
  transfers between devices with their start and end apart: 5 -> 1, of which waited for: 5 -> 1; matrix products, arithmetic and copies ran while one was open for 2% -> 0% of each run, Pallas kernels for 0% -> 0%
where the time goes in v1:
time: 262 us
  waiting for transfers between devices  143 us (55%)
  Pallas kernels  60.6 us (23%)
  blocking collectives  21.2 us (8%)
  between operations  14.2 us (5%)
  matrix products  10 us (4%)
  local copies, waits for them, and re-layouts  9.38 us (4%)
  other arithmetic  3.27 us (1%)
    psum x1, waiting for transfers between devices, on_device(): gram = lax.psum(inner(left, right), ('grp', 'dev'))  143 us
    pallas_call x1, Pallas kernels, cholesky(): pl.pallas_call(cholesky_kernel, out_shape=jax.ShapeDtypeStruct((width, wi...  60.6 us
    psum x1, blocking collectives, on_device(): arcs = lax.psum(inner(jnp.where(onehot, column, 0.0), weighted), 'dev')  21.2 us
    dot_general x2, matrix products, inner(): lax.dot_general(left, right, (((0,), (0,)), ((), ())), precision=lax.Prec...  10 us
  transfers between devices with their start and end apart: 1, of which 1 were waited for; matrix products, arithmetic and copies ran while one was open for 0% of the time, Pallas kernels for 0%

profile of v1, /device:TPU:0, one launch (start us, length us, event | category | flops | bytes accessed | tf_op | source)
XLA Modules:
  0.0 261.8 jit_solution(12689966732380484067)
XLA Ops:
  7.2 0.0 copy-start.1
  7.2 0.0 all-reduce.2.cloned.1.call-start
  7.2 0.9 copy.8
  8.2 1.3 concatenate.12
  9.6 0.0 copy-start.2
  9.6 0.0 copy-done.1
  9.6 2.3 broadcast_multiply_fusion
  11.9 0.7 mul.26
  12.6 0.1 copy.9
  12.8 0.0 copy-done.2
  12.8 0.1 copy.10
  13.0 0.0 copy-start.3
  13.0 2.6 concatenate.13
  15.6 0.0 copy-done.3
  15.6 0.9 fusion.11
  16.5 21.2 %psum.14 = f32[8,1152]{1,0:T(8,128)S(1)} all-reduce(f32[8,1152]{1,0:T(8,128)S(1)} %fusion.11), channel_id=1, replica_groups=mesh['grp'=8,'dev'=4] {'dev'}, use_global_device_ids=true, to_apply=%region_0.1 | all-reduce | flops 9216 | bytes 73728 | tf_op jit(solution)/shard_map/psum | solution.py:157
  37.7 0.2 fusion.17
  37.9 0.1 fusion.16
  38.0 9.2 %fusion = f32[1024,1152]{1,0:T(8,128)} fusion(f32[2,1152]{1,0:T(2,128)S(1)} %constant_dynamic-slice_fusion.2, f32[32,1152]{1,0:T(8,128)S(1)} %constant_dynamic-slice_fusion.3, f32[512,1152]{1,0:T(8,128)S(1)} %concatenate.13, f32[2,1024]{1,0:T(2,128)S(1)} %fusion.16, f32[32,1024]{1,0:T(8,128)S(1)} %constant_dynamic-slice_fusion.1, ...), kind=kOutput, calls=%fused_computation | convolution fusion | flops 3866903040 | bytes 9470976 | tf_op jit(solution)/shard_map/dot_general | solution.py:18
  47.1 0.0 all-reduce.2.cloned.1.call-update
  47.2 143.0 %all-reduce.2.cloned.1.call-done.g_ref = f32[1024,1152]{1,0:T(8,128)} async-done(((f32[1024,1152]{1,0:T(8,128)}), f32[1024,1152]{1,0:T(8,128)}) %all-reduce.2.cloned.1.call-update) | async-done | bytes 4718608 | tf_op jit(solution)/shard_map/psum | solution.py:168
  190.2 0.0 copy-start
  190.2 2.3 copy-done
  192.5 60.6 %shard_map.77 = f32[1024,1152]{1,0:T(8,128)S(1)} custom-call(f32[1024,1152]{1,0:T(8,128)S(1)} %copy-done), custom_call_target="tpu_custom_call" | custom-call | tf_op jit(solution)/shard_map/pallas_call | solution.py:134
  253.1 1.1 constant_dynamic-slice_fusion
  254.2 0.7 dynamic-slice_reduce_fusion
  (5 shorter events, 0.1 us)
Async XLA Ops:
  7.2 2.4 copy-start.1
  7.2 183.0 %all-reduce.2.cloned.1.call-start = ((), (), s32[]{:S(2)}) async-start(), calls=%async_computation | async-start | bytes 9437184 | tf_op jit(solution)/shard_map/psum | solution.py:168
  9.6 3.2 %copy-start.2 = (f32[512]{0:T(512)S(1)}, f32[512]{0:T(512)}, u32[]{:S(2)}) copy-start(f32[512]{0:T(512)} %param.8) | copy-start | bytes 6148
  13.0 2.6 %copy-start.3 = (s32[512,1]{0,1:T(1,128)S(1)}, s32[512,1]{0,1:T(1,128)}, u32[]{:S(2)}) copy-start(s32[512,1]{0,1:T(1,128)} %param.9) | copy-start | bytes 6148
  190.2 2.3 copy-start
Sparse Core Ops, SparseCore 0:
  47.3 142.8 all-reduce.1

commit v2 on v1

--- a/solution.py
+++ b/solution.py
@@ -144,6 +144,148 @@
     )(gram)
 
 
+def packed(gram):
+    width, wide = gram.shape
+    panels = width // BLOCK
+
+    def cut(p):
+        return gram[p * BLOCK : (p + 1) * BLOCK, p * BLOCK :]
+
+    return jnp.concatenate(
+        [
+            jnp.concatenate([cut(p), cut(panels - 1 - p)], axis=1)
+            for p in range(panels // 2)
+        ],
+        axis=0,
+    )
+
+
+def unpacked(pack, width, wide):
+    panels = width // BLOCK
+    rows = []
+    for p in range(panels):
+        q = min(p, panels - 1 - p)
+        size = wide - p * BLOCK
+        at = 0 if p == q else pack.shape[1] - size
+        piece = pack[q * BLOCK : (q + 1) * BLOCK, at : at + size]
+        rows.append(jnp.pad(piece, ((0, 0), (p * BLOCK, 0))))
+    return jnp.concatenate(rows, axis=0)
+
+
+def sum_kernel(orders, cuts, g_ref, out_ref, acc, recv, send_sem, recv_sem, back_send, back_recv):
+    rows = g_ref.shape[0]
+    me = {"grp": lax.axis_index("grp"), "dev": lax.axis_index("dev")}
+
+    def bit_of(axis, bit):
+        return lax.rem(me[axis] // bit, 2)
+
+    def partner(axis, bit):
+        return {axis: me[axis] + bit * (1 - 2 * bit_of(axis, bit))}
+
+    barrier = pltpu.get_barrier_semaphore()
+    for axis, bit in orders[0]:
+        pl.semaphore_signal(
+            barrier, inc=1, device_id=partner(axis, bit), device_id_type=pl.DeviceIdType.MESH
+        )
+    pl.semaphore_wait(barrier, len(orders[0]))
+
+    def add(source, keep, slot, size, lanes):
+        step = min(size, 16)
+
+        def body(i, carry):
+            at = pl.ds(pl.multiple_of(keep + i * step, 8), step)
+            got = pl.ds(pl.multiple_of(slot + i * step, 8), step)
+            acc[at, lanes] = source[at, lanes] + recv[got, lanes]
+            return carry
+
+        lax.fori_loop(0, size // step, body, 0)
+
+    base = [0 for _ in orders]
+    size, slot = rows, 0
+    trail = []
+    for s in range(len(orders[0])):
+        source = g_ref if s == 0 else acc
+        halve = size >= 16
+        part = size // 2 if halve else size
+        copies, keeps = [], []
+        for h, (order, (start, count)) in enumerate(zip(orders, cuts)):
+            axis, bit = order[s]
+            lanes = pl.ds(start, count)
+            mine = bit_of(axis, bit)
+            keep = base[h] + mine * part if halve else base[h]
+            away = base[h] + (1 - mine) * part if halve else base[h]
+            copy = pltpu.make_async_remote_copy(
+                src_ref=source.at[pl.ds(pl.multiple_of(away, 8), part), lanes],
+                dst_ref=recv.at[pl.ds(slot, part), lanes],
+                send_sem=send_sem.at[s, h],
+                recv_sem=recv_sem.at[s, h],
+                device_id=partner(axis, bit),
+                device_id_type=pl.DeviceIdType.MESH,
+            )
+            copy.start()
+            copies.append(copy)
+            keeps.append(keep)
+        for h, (start, count) in enumerate(cuts):
+            copies[h].wait()
+            add(source, keeps[h], slot, part, pl.ds(start, count))
+        if halve:
+            trail.append((s, part))
+        base, size, slot = keeps, part, slot + part
+
+    for h, (start, count) in enumerate(cuts):
+        at = pl.ds(pl.multiple_of(base[h], 8), size)
+        out_ref[at, pl.ds(start, count)] = acc[at, pl.ds(start, count)]
+    for s, part in reversed(trail):
+        copies = []
+        for h, (order, (start, count)) in enumerate(zip(orders, cuts)):
+            axis, bit = order[s]
+            region = out_ref.at[pl.ds(pl.multiple_of(base[h], 8), part), pl.ds(start, count)]
+            copy = pltpu.make_async_remote_copy(
+                src_ref=region,
+                dst_ref=region,
+                send_sem=back_send.at[s, h],
+                recv_sem=back_recv.at[s, h],
+                device_id=partner(axis, bit),
+                device_id_type=pl.DeviceIdType.MESH,
+            )
+            copy.start()
+            copies.append(copy)
+            base[h] = base[h] - bit_of(axis, bit) * part
+        for copy in copies:
+            copy.wait()
+
+
+def sum_all(pack, n_grp, n_dev):
+    rows, lanes = pack.shape
+    grp = [("grp", 1 << i) for i in range(n_grp.bit_length() - 1)]
+    dev = [("dev", 1 << i) for i in range(n_dev.bit_length() - 1)]
+    orders = (grp + dev, grp[:1] + grp[:0:-1] + dev)
+    first = lanes // (2 * BLOCK) * BLOCK
+    cuts = ((0, first), (first, lanes - first))
+    slots, size = 0, rows
+    for _ in orders[0]:
+        size = size // 2 if size >= 16 else size
+        slots += size
+    sems = pltpu.SemaphoreType.DMA((len(orders[0]), 2))
+    return pl.pallas_call(
+        functools.partial(sum_kernel, orders, cuts),
+        out_shape=jax.ShapeDtypeStruct(pack.shape, jnp.float32),
+        in_specs=[pl.BlockSpec(memory_space=pltpu.VMEM)],
+        out_specs=pl.BlockSpec(memory_space=pltpu.VMEM),
+        scratch_shapes=[
+            pltpu.VMEM((rows, lanes), jnp.float32),
+            pltpu.VMEM((slots, lanes), jnp.float32),
+            sems,
+            sems,
+            sems,
+            sems,
+        ],
+        compiler_params=pltpu.CompilerParams(
+            collective_id=0, has_side_effects=True, vmem_limit_bytes=40 * 2**20
+        ),
+    )(pack)
+
+
 def on_device(design, observed, row_weight, arc_of_row, prior_factor, prior_rhs):
     n_dev, n_grp = lax.axis_size("dev"), lax.axis_size("grp")
     dev, grp = lax.axis_index("dev"), lax.axis_index("grp")
@@ -165,7 +307,8 @@
     prior = lax.dynamic_slice_in_dim(prior, grp * prior_rows, prior_rows, 0)
     left = jnp.concatenate([weighted[:, :width], prior[:, :width], -arcs[:, :width] / total], axis=0)
     right = jnp.concatenate([weighted, prior, arcs], axis=0)
-    gram = lax.psum(inner(left, right), ("grp", "dev"))
+    pack = sum_all(packed(inner(left, right)), n_grp, n_dev)
+    gram = unpacked(pack, width, width + BLOCK)
     factor = cholesky(gram)
     share = width // n_dev
     rows = lax.dynamic_slice_in_dim(factor, dev * share, share, 0)

time: 262 us -> 165 us (0.63)
  waiting for transfers between devices: 143 us -> 0 us
  Pallas kernels: 60.6 us -> 119 us
  between operations: 14.2 us -> 0.96 us
    psum x1 -> x0, waiting for transfers between devices: 143 us -> none  [on_device(): gram = lax.psum(inner(left, right), ('grp', 'dev'))]
    pallas_call x0 -> x1, Pallas kernels: none -> 58.3 us  [sum_all(): pl.pallas_call(functools.partial(sum_kernel, orders, cuts), out_shape=jax...]
  transfers between devices with their start and end apart: 1 -> 0, of which waited for: 1 -> 0; matrix products, arithmetic and copies ran while one was open for 0% -> 0% of each run, Pallas kernels for 0% -> 0%
where the time goes in v2:
time: 165 us
  Pallas kernels  119 us (72%)
  blocking collectives  21.2 us (13%)
  local copies, waits for them, and re-layouts  11.8 us (7%)
  matrix products  8.84 us (5%)
  other arithmetic  2.87 us (2%)
    pallas_call x1, Pallas kernels, cholesky(): pl.pallas_call(cholesky_kernel, out_shape=jax.ShapeDtypeStruct((width, wi...  60.8 us
    pallas_call x1, Pallas kernels, sum_all(): pl.pallas_call(functools.partial(sum_kernel, orders, cuts), out_shape=jax...  58.3 us
    psum x1, blocking collectives, on_device(): arcs = lax.psum(inner(jnp.where(onehot, column, 0.0), weighted), 'dev')  21.2 us
    dot_general x2, matrix products, inner(): lax.dot_general(left, right, (((0,), (0,)), ((), ())), precision=lax.Prec...  8.84 us

profile of v2, /device:TPU:0, one launch (start us, length us, event | category | flops | bytes accessed | tf_op | source)
XLA Modules:
  0.0 164.8 jit_solution(6341025019328809787)
XLA Ops:
  0.6 0.0 copy-start.4
  0.6 0.0 copy-start
  0.7 0.8 mul.26
  1.5 1.5 copy.8
  3.0 0.1 copy.9
  3.1 1.5 copy.10
  4.7 0.7 broadcast_in_dim.27
  5.3 1.4 concatenate.30
  6.7 0.7 constant_dynamic-slice_fusion.1
  7.4 0.7 constant_dynamic-slice_fusion.3
  8.1 0.0 copy-done.4
  8.1 0.0 copy-done
  8.1 0.0 copy-start.1
  8.1 1.6 broadcast_multiply_fusion
  9.6 0.0 copy-start.5
  9.7 0.0 copy-done.1
  9.7 0.0 copy-start.2
  9.7 0.0 copy-start.3
  9.7 2.7 %concatenate.31 = f32[512,1152]{1,0:T(8,128)S(1)} concatenate(f32[512,1024]{1,0:T(8,128)} %broadcast_multiply_fusion, f32[512,1]{1,0:T(8,128)S(1)} %copy.9, f32[512,1]{1,0:T(8,128)S(1)} %copy-done.1, f32[512,126]{1,0:T(8,128)S(1)} %broadcast_in_dim.31), dimensions={1} | concatenate | bytes 4718592 | tf_op jit(solution)/shard_map/concatenate | solution.py:297
  12.4 0.0 copy-done.5
  12.4 0.9 fusion.11
  13.3 21.2 %psum.7 = f32[8,1152]{1,0:T(8,128)S(1)} all-reduce(f32[8,1152]{1,0:T(8,128)S(1)} %fusion.11), channel_id=1, replica_groups=mesh['grp'=8,'dev'=4] {'dev'}, use_global_device_ids=true, to_apply=%region_0.1 | all-reduce | flops 9216 | bytes 73728 | tf_op jit(solution)/shard_map/psum | solution.py:299
  34.5 0.2 fusion.17
  34.7 0.1 fusion.16
  34.8 0.0 copy-done.2
  34.8 0.0 copy-done.3
  34.8 8.0 %fusion = f32[1024,1152]{1,0:T(8,128)S(1)} fusion(f32[2,1152]{1,0:T(2,128)S(1)} %constant_dynamic-slice_fusion.2, f32[32,1152]{1,0:T(8,128)S(1)} %copy-done.2, f32[512,1152]{1,0:T(8,128)S(1)} %concatenate.31, f32[2,1024]{1,0:T(2,128)S(1)} %fusion.16, f32[32,1024]{1,0:T(8,128)S(1)} %copy-done.3, f32[512,1024]{1,0:T(8,128)} %broadcast_multiply_fusion), kind=kOutput, calls=%fused_computation.1 | convolution fusion | flops 3866903040 | bytes 9470976 | tf_op jit(solution)/shard_map/dot_general | solution.py:18
  43.0 0.2 maximum_maximum_fusion.g_ref
  43.2 58.3 %shard_map.77 = f32[512,1408]{1,0:T(8,128)S(1)} custom-call(f32[512,1408]{1,0:T(8,128)S(1)} %maximum_maximum_fusion.g_ref), custom_call_target="tpu_custom_call" | custom-call | tf_op jit(solution)/shard_map/pallas_call | solution.py:270
  102.2 60.8 %shard_map.78 = f32[1024,1152]{1,0:T(8,128)S(1)} custom-call(f32[1024,1152]{1,0:T(8,128)S(1)} %pad_dynamic-update-slice_fusion.g_ref), custom_call_target="tpu_custom_call" | custom-call | tf_op jit(solution)/shard_map/pallas_call | solution.py:134
  163.0 0.7 dynamic-slice_reduce_fusion
  163.7 1.1 constant_dynamic-slice_fusion
  (25 shorter events, 0.7 us)
Async XLA Ops:
  0.6 7.4 %copy-start.4 = (f32[512]{0:T(512)S(1)}, f32[512]{0:T(512)}, u32[]{:S(2)}) copy-start(f32[512]{0:T(512)} %param.8) | copy-start | bytes 6148
  0.6 7.4 %copy-start = (f32[512,1024]{1,0:T(8,128)S(1)}, f32[512,1024]{1,0:T(8,128)}, u32[]{:S(2)}) copy-start(f32[512,1024]{1,0:T(8,128)} %param.6) | copy-start | bytes 6291460
  8.1 1.6 copy-start.1
  9.6 2.8 %copy-start.5 = (s32[512,1]{0,1:T(1,128)S(1)}, s32[512,1]{0,1:T(1,128)}, u32[]{:S(2)}) copy-start(s32[512,1]{0,1:T(1,128)} %param.9) | copy-start | bytes 6148
  9.7 25.1 %copy-start.2 = (f32[32,1152]{1,0:T(8,128)S(1)}, f32[32,1152]{1,0:T(8,128)}, u32[]{:S(2)}) copy-start(f32[32,1152]{1,0:T(8,128)} %constant_dynamic-slice_fusion.3) | copy-start | bytes 442372
  9.7 25.1 %copy-start.3 = (f32[32,1024]{1,0:T(8,128)S(1)}, f32[32,1024]{1,0:T(8,128)}, u32[]{:S(2)}) copy-start(f32[32,1024]{1,0:T(8,128)} %constant_dynamic-slice_fusion.1) | copy-start | bytes 393220
